TPU v7x, 512 devices: a whole 4x4x16 slice. The times are simulated.
512 devices in a mesh: tok: 128 (over z_lo, x, y), mem: 4 (over z_hi, core).
Axes of the slice: x: 4, y: 4, z: 16 (z_hi: 2, z_lo: 8; z = z_hi * 8 + z_lo), core: 2. Of those that a mesh axis runs over, the one named last changes fastest.
Arguments:
- query_states: bfloat16 [4, 32768, 1024], P('mem', 'tok'), may hold values from -8 to 8
- key_states: bfloat16 [4, 32768, 1024], P('mem', 'tok'), may hold values from -8 to 8
- value_states: bfloat16 [4, 32768, 1024], P('mem', 'tok'), may hold values from -6 to 6
- observed: bfloat16 [32768, 1024], P('tok'), may hold values from -8 to 8
- closing_projector: bfloat16 [1024, 1024], P(('tok', 'mem')), may hold values from -0.1875 to 0.1875
Outputs:
- grad_query: bfloat16 [4, 32768, 1024], P('mem', 'tok')
- grad_key: bfloat16 [4, 32768, 1024], P('mem', 'tok')
- grad_value: bfloat16 [4, 32768, 1024], P('mem', 'tok')
All inputs are finite; a program needn't handle non-finite values.
Results may differ from a plain program's by a relative error of at most 0.035.
Values may be sent and summed in bfloat16 or wider, within the bound.
A program may use at most 128 MiB of HBM per device.

v0:
```python
import math

import jax
import jax.numpy as jnp
from jax import lax
from jax.sharding import PartitionSpec as P

HEADS = 16
REACH = 128


def extended(shard, sides, width):
    for axis, dim in sides:
        size, length = (lax.axis_size(axis), shard.shape[dim])
        up = [(i, (i + 1) % size) for i in range(size - 1)]
        down = [(j, i) for i, j in up]
        last = lax.slice_in_dim(shard, length - width, length, axis=dim)
        first = lax.slice_in_dim(shard, 0, width, axis=dim)
        before = lax.ppermute(last, axis, up)
        after = lax.ppermute(first, axis, down)
        shard = jnp.concatenate([before, shard, after], axis=dim)
    return shard


def from_behind(block, axis, distance):
    devices = range(lax.axis_size(axis))
    route = [(i - distance, i) for i in devices if i - distance in devices]
    return lax.ppermute(block, axis, route)


def score_derivative(difference):
    return difference / jnp.sqrt(difference * difference + 0.25)


def body(query_states, key_states, value_states, observed, closing_projector):
    tok_rows = query_states.shape[1]
    model_width = query_states.shape[2]
    head_size = model_width // HEADS
    key_span = tok_rows + 2 * REACH
    score_scale = 1.0 / math.sqrt(head_size)
    members = lax.axis_size("mem")
    tok_place = lax.axis_index("tok")
    total_tokens = tok_rows * lax.axis_size("tok")
    area_weights = lax.all_gather(closing_projector, ("tok", "mem"), axis=0, tiled=True)
    stacked = jnp.stack([key_states[0], value_states[0]])
    window = extended(stacked, (("tok", 1),), REACH)
    key_heads = window[0].reshape(key_span, HEADS, head_size)
    value_heads = window[1].reshape(key_span, HEADS, head_size)
    query_heads = query_states[0].reshape(tok_rows, HEADS, head_size)
    relative = (
        jnp.arange(key_span, dtype=jnp.int32)[None, :]
        - REACH
        - jnp.arange(tok_rows, dtype=jnp.int32)[:, None]
    )
    position = tok_place * tok_rows + jnp.arange(key_span, dtype=jnp.int32) - REACH
    inside = (position >= 0) & (position < total_tokens)
    window_weight = jnp.where((jnp.abs(relative) <= REACH) & inside[None, :], 1.0, 0.0).astype(
        jnp.float32
    )
    scores = (
        jnp.einsum("ihd,jhd->hij", query_heads, key_heads, preferred_element_type=jnp.float32)
        * score_scale
    )
    masked = jnp.where(window_weight[None] > 0, scores, -jnp.inf)
    row_max = jnp.max(masked, axis=-1, keepdims=True)
    scaled = window_weight[None] * jnp.exp(masked - row_max)
    row_total = jnp.sum(scaled, axis=-1, keepdims=True)
    attn_prob = scaled / row_total
    prob_low = attn_prob.astype(jnp.bfloat16)
    mixed_context = jnp.einsum(
        "hij,jhd->ihd", prob_low, value_heads, preferred_element_type=jnp.float32
    )
    mixed_context = mixed_context.reshape(tok_rows, model_width).astype(jnp.bfloat16)
    predicted_latent = jnp.dot(
        mixed_context, area_weights, preferred_element_type=jnp.float32
    ).astype(jnp.bfloat16)
    whole_cohort = lax.all_gather(predicted_latent[None], "mem", axis=0, tiled=True).astype(
        jnp.float32
    )
    resident_portion = predicted_latent.astype(jnp.float32)
    couple_contributions = jnp.sum(score_derivative(resident_portion[None] - whole_cohort), axis=0)
    truth_analysis = observed.astype(jnp.float32)
    prediction_adjoint = (
        score_derivative(resident_portion - truth_analysis) - couple_contributions / (members - 1)
    ).astype(jnp.bfloat16)
    attended_grad = lax.dot_general(
        prediction_adjoint,
        area_weights,
        (((1,), (1,)), ((), ())),
        preferred_element_type=jnp.float32,
    ).astype(jnp.bfloat16)
    grad_heads = attended_grad.reshape(tok_rows, HEADS, head_size)
    prob_grad = jnp.einsum(
        "ihd,jhd->hij", grad_heads, value_heads, preferred_element_type=jnp.float32
    )
    row_dot = jnp.sum(attn_prob * prob_grad, axis=-1, keepdims=True)
    score_grad = (attn_prob * (prob_grad - row_dot) * score_scale).astype(jnp.bfloat16)
    query_grad = jnp.einsum(
        "hij,jhd->ihd", score_grad, key_heads, preferred_element_type=jnp.float32
    )
    query_grad = query_grad.reshape(tok_rows, model_width).astype(jnp.bfloat16)
    key_terms = jnp.einsum(
        "hij,ihd->jhd", score_grad, query_heads, preferred_element_type=jnp.float32
    )
    value_terms = jnp.einsum(
        "hij,ihd->jhd", prob_low, grad_heads, preferred_element_type=jnp.float32
    )
    both_terms = jnp.stack(
        [key_terms.reshape(key_span, model_width), value_terms.reshape(key_span, model_width)]
    )
    from_above = from_behind(both_terms[:, :REACH].astype(jnp.bfloat16), "tok", -1).astype(
        jnp.float32
    )
    from_below = from_behind(
        both_terms[:, REACH + tok_rows :].astype(jnp.bfloat16), "tok", 1
    ).astype(jnp.float32)
    centre = both_terms[:, REACH : REACH + tok_rows]
    centre = centre.at[:, tok_rows - REACH :].add(from_above)
    centre = centre.at[:, :REACH].add(from_below)
    grad_key = centre[0].astype(jnp.bfloat16)
    grad_value = centre[1].astype(jnp.bfloat16)
    return (query_grad[None], grad_key[None], grad_value[None])


def solution(mesh):
    placed = (
        P("mem", "tok", None),
        P("mem", "tok", None),
        P("mem", "tok", None),
        P("tok", None),
        P(("tok", "mem"), None),
    )
    return jax.shard_map(
        body,
        mesh=mesh,
        in_specs=placed,
        out_specs=(P("mem", "tok", None), P("mem", "tok", None), P("mem", "tok", None)),
        check_vma=False,
    )
```

profile of v0, /device:TPU:126, one launch (start us, length us, event | category | flops | bytes accessed | tf_op | source)
XLA Modules:
  0.0 925.4 jit_solution(4099840420042414163)
XLA Ops:
  10.2 2.7 collective-permute-start.1
  12.9 8.6 collective-permute-start
  23.8 7.4 collective-permute-done.1
  34.9 7.5 fusion.58
  42.4 5.0 fusion.26
  47.4 720.6 %all-gather.7.cloned.1.call-done = bf16[512,2,1024]{2,1,0:T(2,128)(2,1)} async-done(((bf16[1,2,1024]{2,1,0:T(2,128)(2,1)}), bf16[512,2,1024]{2,1,0:T(2,128)(2,1)}) %all-gather.7.cloned.1.call-update) | async-done | bytes 2097168 | tf_op jit(solution)/shard_map/all_gather | solution.py:44
  768.0 2.7 reshape.176
  770.7 2.9 fusion.59
  773.7 73.6 %all-gather.5.cloned.1.call-done = bf16[1024,1024]{1,0:T(8,128)(2,1)} async-done(((bf16[256,1024]{1,0:T(8,128)(2,1)}), bf16[1024,1024]{1,0:T(8,128)(2,1)}) %all-gather.5.cloned.1.call-update) | async-done | bytes 2097168 | tf_op jit(solution)/shard_map/all_gather | solution.py:77
  847.3 3.0 fusion.11
  850.3 1.7 convolution_convert_fusion
  852.1 1.2 copy.40
  853.3 4.5 fusion.60
  857.8 6.1 fusion.22
  864.0 13.5 %fusion.16 = f32[16,512,64]{1,2,0:T(8,128)} fusion(bf16[256,16,64]{0,2,1:T(8,128)(2,1)S(1)} %bitcast.53, f32[16,256,512]{1,2,0:T(8,128)} %fusion.60, f32[16,256,512]{1,2,0:T(8,128)} %get-tuple-element.45, f32[16,256]{1,0:T(8,128)S(1)} %get-tuple-element.44), kind=kOutput, calls=%fused_computation.24 | convolution fusion | flops 283120128 | bytes 19415040 | tf_op jit(solution)/shard_map/hij,ihd->jhd/dot_general | solution.py:102
  877.4 1.9 copy.46
  879.4 2.9 copy.47
  882.3 2.0 fusion.6
  885.4 2.7 collective-permute-start.2
  888.1 8.7 collective-permute-start.3
  896.9 14.0 %fusion.29 = bf16[16,64,256]{2,1,0:T(8,128)(2,1)} fusion(bf16[512,16,64]{0,2,1:T(8,128)(2,1)S(1)} %bitcast.51, f32[16,256,512]{1,2,0:T(8,128)} %fusion.60, f32[16,256,512]{1,2,0:T(8,128)} %get-tuple-element.45, f32[16,256]{1,0:T(8,128)S(1)} %get-tuple-element.44), kind=kOutput, calls=%fused_computation.35 | convolution fusion | flops 283382272 | bytes 18366464 | tf_op jit(solution)/shard_map/hij,jhd->ihd/dot_general | solution.py:98
  910.9 2.0 copy.48
  912.9 1.6 fusion.21
  916.0 1.3 fusion.35
  (37 shorter events, 12.8 us)
Async XLA Ops:
  7.2 14.3 %copy-start.4 = (bf16[1,256,1024]{2,1,0:T(8,128)(2,1)S(1)}, bf16[1,256,1024]{2,1,0:T(8,128)(2,1)}, u32[]{:S(2)}) copy-start(bf16[1,256,1024]{2,1,0:T(8,128)(2,1)} %param.9) | copy-start | bytes 1572868
  7.2 760.8 %all-gather.7.cloned.1.call-start = ((), (), s32[]{:S(2)}) async-start(), calls=%async_computation.1 | async-start | bytes 2101248 | tf_op jit(solution)/shard_map/all_gather | solution.py:44
  7.9 839.4 %all-gather.5.cloned.1.call-start = ((), (), s32[]{:S(2)}) async-start(), calls=%async_computation | async-start | bytes 2621440 | tf_op jit(solution)/shard_map/all_gather | solution.py:77
  10.2 21.0 %collective-permute-start.1 = (bf16[2,128,1024]{2,1,0:T(8,128)(2,1)S(1)}, bf16[2,128,1024]{2,1,0:T(8,128)(2,1)S(1)}, u32[]{:S(2)}, u32[]{:S(2)}) collective-permute-start(bf16[2,128,1024]{2,1,0:T(8,128)(2,1)S(1)} %get-tuple-element.43), channel_id=1, source_target_pairs={{4,0},{8,4},{12,8},{16,12},{20,16},{24,20},{28,24},{32,28},{36,32}... | collective-permute-start | bytes 1572872 | tf_op jit(solution)/shard_map/ppermute | solution.py:20
  12.9 19.5 %collective-permute-start = (bf16[2,128,1024]{2,1,0:T(8,128)(2,1)S(1)}, bf16[2,128,1024]{2,1,0:T(8,128)(2,1)}, u32[]{:S(2)}, u32[]{:S(2)}) collective-permute-start(bf16[2,128,1024]{2,1,0:T(8,128)(2,1)S(1)} %get-tuple-element.42), channel_id=1, source_target_pairs={{0,4},{4,8},{8,12},{12,16},{16,20},{20,24},{24,28},{28,32},{32,36}... | collective-permute-start | bytes 1572872 | tf_op jit(solution)/shard_map/ppermute | solution.py:19
  34.3 8.0 copy-start.2
  847.3 3.0 copy-start.1
  847.3 3.0 copy-start.6
  857.8 6.1 copy-start.5
  882.3 14.5 %copy-start.3 = (bf16[1,512,1024]{1,2,0:T(8,128)(2,1)S(1)}, bf16[1,512,1024]{1,2,0:T(8,128)(2,1)}, u32[]{:S(2)}) copy-start(bf16[1,512,1024]{1,2,0:T(8,128)(2,1)} %copy-done.2) | copy-start | bytes 3145732
  885.4 29.1 %collective-permute-start.2 = (bf16[2,128,1024]{2,1,0:T(8,128)(2,1)}, bf16[2,128,1024]{2,1,0:T(8,128)(2,1)}, u32[]{:S(2)}, u32[]{:S(2)}) collective-permute-start(bf16[2,128,1024]{2,1,0:T(8,128)(2,1)} %get-tuple-element.37), channel_id=1, source_target_pairs={{4,0},{8,4},{12,8},{16,12},{20,16},{24,20},{28,24},{32,28},{36,32}... | collective-permute-start | bytes 1572872 | tf_op jit(solution)/shard_map/ppermute | solution.py:28
  888.1 27.9 %collective-permute-start.3 = (bf16[2,128,1024]{2,1,0:T(8,128)(2,1)}, bf16[2,128,1024]{2,1,0:T(8,128)(2,1)}, u32[]{:S(2)}, u32[]{:S(2)}) collective-permute-start(bf16[2,128,1024]{2,1,0:T(8,128)(2,1)} %get-tuple-element.36), channel_id=1, source_target_pairs={{0,4},{4,8},{8,12},{12,16},{16,20},{20,24},{24,28},{28,32},{32,36}... | collective-permute-start | bytes 1572872 | tf_op jit(solution)/shard_map/ppermute | solution.py:28
  912.9 1.9 copy-start
Sparse Core Ops, SparseCore 0:
  10.1 757.8 all-gather.6
  773.8 73.4 all-gather.4
where the time goes:
time: 926 us; the launch traced here: 925 us
  waiting for transfers between devices  803 us (87%)
  matrix products  55.3 us (6%)
  starting transfers between devices  22.8 us (2%)
  local copies, waits for them, and re-layouts  17.8 us (2%)
  between operations  14.3 us (2%)
  other arithmetic  11.8 us (1%)
    all_gather x1, waiting for transfers between devices, body(): lax.all_gather(closing_projector, ('tok', 'mem'), axis=0, tiled=True)  721 us
    all_gather x1, waiting for transfers between devices, body(): lax.all_gather(predicted_latent[None], 'mem', axis=0, tiled=True)  73.6 us
  transfers between devices with their start and end apart: 6, of which 4 were waited for; matrix products, arithmetic and copies ran while one was open for 4% of the time, Pallas kernels for 0%

commit v1 on v0

v1 whole, which is shorter than its diff:
```python
import jax
import jax.numpy as jnp
from jax import lax
from jax.experimental import pallas as pl
from jax.experimental.pallas import tpu as pltpu
from jax.sharding import PartitionSpec as P

MESH = pl.DeviceIdType.MESH
F32 = jnp.float32
BF16 = jnp.bfloat16

TOK = 128
ROWS = 256
REACH = 128
WIDTH = 1024
HD = 64
TILE = 64
TILES = 4
WIN = TILE + 2 * REACH
LANES = 256
QUADS = 4
EXT = ROWS + 2 * REACH
BLOCKED = -1e30


def chip(x, y, z, c):
    return ((z % 8) * 16 + x * 4 + y, (z // 8) * 2 + c)


def dot(a, b, ca, cb):
    return lax.dot_general(a, b, (((ca,), (cb,)), ((), ())), preferred_element_type=F32)


def slope(d):
    return d * lax.rsqrt(d * d + 0.25)


def lanes_of(quad):
    return pl.ds(pl.multiple_of(quad * LANES, LANES), LANES)


def kernel(
    q_hbm, k_hbm, v_hbm, o_hbm, w_in,
    gq_hbm, gk_hbm, gv_hbm,
    q_s, kx, vx, obs, w_tmp, wg, wf, w_s, att, probs, rl_rows, rl_lanes, bias,
    dout, acc_k, acc_v, sbuf, rbuf, gq_s, gk_s, gv_s,
    load_sem, halo_ss, halo_rs, wz_ss, wz_rs, wn_ss, wn_rs, wy_ss, wy_rs, wx_ss, wx_rs, wc_ss, wc_rs,
    far_ss, far_rs, sib_ss, sib_rs, fwd_ss, fwd_rs, ret_ss, ret_rs, out_sem,
):
    tok = lax.axis_index("tok")
    mem = lax.axis_index("mem")
    x = (tok // 4) % 4
    y = tok % 4
    z = (mem // 2) * 8 + tok // 16
    c = mem % 2
    sibling = (tok, (mem // 2) * 2 + (1 - c))
    far = (tok, (mem + 2) % 4)
    lower = (tok - 1, mem)
    upper = (tok + 1, mem)
    has_lower = tok > 0
    has_upper = tok < TOK - 1

    def remote(src, dst, ss, rs, device):
        return pltpu.make_async_remote_copy(
            src_ref=src, dst_ref=dst, send_sem=ss, recv_sem=rs, device_id=device, device_id_type=MESH
        )

    barrier = pltpu.get_barrier_semaphore()

    def greet(device):
        pl.semaphore_signal(barrier, inc=1, device_id=device, device_id_type=MESH)

    greet(sibling)
    for d in (1, 2, 3):
        greet(chip(x, y, (z + 4 * d) % 16, c))
        greet(chip(x, y, (z + 16 - d) % 16, c))
        greet(chip(x, (y + d) % 4, z, c))
        greet(chip((x + d) % 4, y, z, c))

    @pl.when(has_lower)
    def _():
        greet(lower)

    @pl.when(has_upper)
    def _():
        greet(upper)

    own = pl.ds(REACH, ROWS)
    loads = [
        pltpu.make_async_copy(k_hbm.at[0], kx.at[own], load_sem.at[0]),
        pltpu.make_async_copy(q_hbm.at[0], q_s, load_sem.at[1]),
        pltpu.make_async_copy(v_hbm.at[0], vx.at[own], load_sem.at[2]),
        pltpu.make_async_copy(o_hbm, obs, load_sem.at[3]),
    ]
    for cp in loads:
        cp.start()

    mine = w_in[...].astype(F32)
    for r in range(2):
        for b in range(8):
            w_tmp[r * 8 + b : r * 8 + b + 1, :] = mine[r : r + 1, b * 128 : (b + 1) * 128]
    unit = ((c * 4 + x) * 4 + y) * 16 + (z % 4) * 4 + z // 4
    wg[unit] = w_tmp[...].astype(BF16)

    pl.semaphore_wait(
        barrier, 13 + jnp.where(has_lower, 1, 0) + jnp.where(has_upper, 1, 0)
    )

    def halo(side, kv, quad):
        src = (k_hbm, v_hbm)[kv]
        dst = (kx, vx)[kv]
        cols = lanes_of(quad)
        if side == 0:
            return remote(
                src.at[0, pl.ds(ROWS - REACH, REACH), cols], dst.at[pl.ds(0, REACH), cols],
                halo_ss.at[0, kv, quad], halo_rs.at[0, kv, quad], upper,
            )
        return remote(
            src.at[0, pl.ds(0, REACH), cols], dst.at[pl.ds(REACH + ROWS, REACH), cols],
            halo_ss.at[1, kv, quad], halo_rs.at[1, kv, quad], lower,
        )

    def start_halo(quad, carry):
        @pl.when(has_upper)
        def _():
            halo(0, 0, quad).start()
            halo(0, 1, quad).start()

        @pl.when(has_lower)
        def _():
            halo(1, 0, quad).start()
            halo(1, 1, quad).start()

        return carry

    lax.fori_loop(0, QUADS, start_halo, 0)

    def w_copy(first, count, ss, rs, device):
        block = wg.at[pl.ds(first, count)]
        return remote(block, block, ss, rs, device)

    def w_step(step, d, incoming):
        away = (z + 16 - 4 * d) % 16 if step == 0 else (z + 16 - d) % 16
        away = away if incoming else z
        plane = ((c * 4 + x) * 4 + y) * 16
        if step == 0:
            return w_copy(
                plane + (away % 4) * 4 + away // 4, 1, wz_ss.at[d - 1], wz_rs.at[d - 1],
                chip(x, y, (z + 4 * d) % 16, c),
            )
        if step == 1:
            return w_copy(
                plane + (away % 4) * 4, 4, wn_ss.at[d - 1], wn_rs.at[d - 1], chip(x, y, (z + d) % 16, c)
            )
        if step == 2:
            column = (y + 4 - d) % 4 if incoming else y
            return w_copy(
                ((c * 4 + x) * 4 + column) * 16, 16, wy_ss.at[d - 1], wy_rs.at[d - 1],
                chip(x, (y + d) % 4, z, c),
            )
        column = (x + 4 - d) % 4 if incoming else x
        return w_copy(
            (c * 4 + column) * 64, 64, wx_ss.at[d - 1], wx_rs.at[d - 1], chip((x + d) % 4, y, z, c)
        )

    def w_start(step):
        for d in (1, 2, 3):
            w_step(step, d, False).start()

    def w_wait(step):
        for d in (1, 2, 3):
            w_step(step, d, True).wait_recv()

    def w_sent(step):
        for d in (1, 2, 3):
            w_step(step, d, False).wait_send()

    w_sib_out = w_copy(c * 256, 256, wc_ss, wc_rs, sibling)
    w_sib_in = w_copy((1 - c) * 256, 256, wc_ss, wc_rs, sibling)

    w_start(0)

    row = lax.broadcasted_iota(jnp.int32, (WIN, LANES), 0)
    query = lax.broadcasted_iota(jnp.int32, (WIN, LANES), 1) % TILE
    band = (row >= query) & (row <= query + 2 * REACH)
    for t in range(TILES):
        place = row + TILE * t
        lowest = jnp.where(has_lower, 0, REACH)
        highest = jnp.where(has_upper, EXT, REACH + ROWS)
        inside = (place >= lowest) & (place < highest)
        bias[t] = jnp.where(band & inside, 0.0, BLOCKED)

    def zero(i, carry):
        rows = pl.ds(pl.multiple_of(i * 32, 32), 32)
        acc_k[rows, :] = jnp.zeros((32, WIDTH), F32)
        acc_v[rows, :] = jnp.zeros((32, WIDTH), F32)
        return carry

    lax.fori_loop(0, EXT // 32, zero, 0)

    @pl.when(jnp.logical_not(has_lower))
    def _():
        kx[pl.ds(0, REACH), :] = jnp.zeros((REACH, WIDTH), BF16)
        vx[pl.ds(0, REACH), :] = jnp.zeros((REACH, WIDTH), BF16)
        for slot in (1, 3):
            rbuf[slot] = jnp.zeros((2, TILE, WIDTH), BF16)

    @pl.when(jnp.logical_not(has_upper))
    def _():
        kx[pl.ds(REACH + ROWS, REACH), :] = jnp.zeros((REACH, WIDTH), BF16)
        vx[pl.ds(REACH + ROWS, REACH), :] = jnp.zeros((REACH, WIDTH), BF16)
        for slot in (0, 2):
            rbuf[slot] = jnp.zeros((2, TILE, WIDTH), BF16)

    for cp in loads:
        cp.wait()

    left_half = lax.broadcasted_iota(jnp.int32, (TILE, 128), 1) < HD

    def spread(pairs):
        none = jnp.zeros((TILE, 128), F32)
        rows = []
        for h in range(4):
            keep = left_half if h % 2 == 0 else jnp.logical_not(left_half)
            part = jnp.where(keep, pairs[h], 0.0)
            rows.append(jnp.concatenate([part, none] if h < 2 else [none, part], axis=1))
        return jnp.concatenate(rows, axis=0).astype(BF16)

    def tile_of(i):
        return i // 2 + (i % 2) * (3 - 2 * (i // 2))

    def query_block(t, quad):
        rows = pl.ds(pl.multiple_of(t * TILE, TILE), TILE)
        part = q_s[rows, lanes_of(quad)].astype(F32) * 0.125
        return spread([part[:, :128], part[:, :128], part[:, 128:], part[:, 128:]])

    def far_copy(i, quad):
        cols = lanes_of(quad)
        return remote(att.at[0, i, :, cols], att.at[2, i, :, cols], far_ss.at[i, quad], far_rs.at[i, quad], far)

    def fwd_copy(i, quad):
        cols = lanes_of(quad)
        return remote(att.at[2, i, :, cols], att.at[3, i, :, cols], fwd_ss.at[i, quad], fwd_rs.at[i, quad], sibling)

    def sib_copy(i):
        return remote(att.at[0, i], att.at[1, i], sib_ss.at[i], sib_rs.at[i], sibling)

    ones = jnp.ones((WIN, 128), BF16)

    def forward_quad(i, quad):
        t = tile_of(i)

        @pl.when((i == 0) & has_lower)
        def _():
            halo(0, 0, quad).wait_recv()
            halo(0, 1, quad).wait_recv()

        @pl.when((i == 1) & has_upper)
        def _():
            halo(1, 0, quad).wait_recv()
            halo(1, 1, quad).wait_recv()

        cols = lanes_of(quad)
        window = pl.ds(pl.multiple_of(t * TILE, TILE), WIN)
        scores = dot(kx[window, cols], query_block(t, quad), 1, 1) + bias[t]
        top = jnp.max(scores, axis=0, keepdims=True)
        weights = jnp.exp(scores - top).astype(BF16)
        total = jnp.sum(weights.astype(F32), axis=0, keepdims=True)
        n = i * QUADS + quad
        probs[n] = weights
        rl_lanes[n] = jnp.broadcast_to(1.0 / total, (8, LANES))
        values = vx[window, cols]
        halves = []
        for half in range(2):
            part = slice(half * 128, half * 128 + 128)
            rhs = jnp.concatenate([values[:, part], ones], axis=1)
            mixed = dot(weights[:, part], rhs, 0, 0)
            inverse = 1.0 / mixed[:, 128:]
            rl_rows[n, pl.ds(half * 128, 128), :] = inverse
            mixed = mixed[:, :128] * inverse
            halves.append(jnp.where(left_half, mixed[:TILE], mixed[TILE:]))
        att[0, i, :, cols] = jnp.concatenate(halves, axis=1).astype(BF16)
        far_copy(i, quad).start()

    def forward_tile(i, carry):
        def step(quad, inner):
            forward_quad(i, quad)
            return inner

        lax.fori_loop(0, QUADS, step, 0)
        sib_copy(i).start()

        @pl.when(i == 0)
        def _():
            w_wait(0)
            w_start(1)

        @pl.when(i == 1)
        def _():
            w_wait(1)
            w_start(2)

        @pl.when(i == 2)
        def _():
            w_wait(2)
            w_start(3)

        return carry

    lax.fori_loop(0, TILES, forward_tile, 0)

    w_wait(3)
    w_sib_out.start()
    w_sib_in.wait_recv()

    def place_units(n, carry):
        for zr in range(4):
            for zq in range(4):
                d = ((zq % 2) * 4 + zr) * 64 + (n % 16) * 4 + (zq // 2) * 2 + n // 16
                wf[pl.ds(pl.multiple_of(d * 16, 16), 16), :] = wg[n * 16 + zr * 4 + zq].astype(F32)
        return carry

    lax.fori_loop(0, 32, place_units, 0)

    def place_rows(n, carry):
        rows = pl.ds(pl.multiple_of(n * 128, 128), 128)
        for b in range(8):
            part = wf[pl.ds(n * 1024 + b, 128, stride=8), :]
            w_s[rows, b * 128 : (b + 1) * 128] = part.astype(BF16)
        return carry

    lax.fori_loop(0, 8, place_rows, 0)

    def return_copy(i, kv, quad, device):
        cols = lanes_of(quad)
        return remote(sbuf.at[i, kv, :, cols], rbuf.at[i, kv, :, cols], ret_ss.at[i, kv, quad], ret_rs.at[i, kv, quad], device)

    def backward_quad(i, quad):
        t = tile_of(i)
        cols = lanes_of(quad)
        window = pl.ds(pl.multiple_of(t * TILE, TILE), WIN)
        n = i * QUADS + quad
        part = dout[:, cols].astype(F32)
        pairs = [part[:, :128], part[:, :128], part[:, 128:], part[:, 128:]]
        grads = spread([pairs[h] * rl_rows[n, h * TILE : (h + 1) * TILE, :] for h in range(4)])
        weights = probs[n]
        prob_grad = dot(vx[window, cols], grads, 1, 1)
        wide = weights.astype(F32)
        row_dot = jnp.sum(wide * prob_grad, axis=0, keepdims=True) * rl_lanes[n, 0:1, :]
        score_grad = (wide * (prob_grad - row_dot)).astype(BF16)
        keys = kx[window, cols]
        halves = []
        for half in range(2):
            side = slice(half * 128, half * 128 + 128)
            mixed = dot(score_grad[:, side], keys[:, side], 0, 0) * 0.125
            halves.append(jnp.where(left_half, mixed[:TILE], mixed[TILE:]))
        rows = pl.ds(pl.multiple_of(t * TILE, TILE), TILE)
        gq_s[rows, cols] = jnp.concatenate(halves, axis=1).astype(BF16)
        acc_k[window, cols] += dot(score_grad, query_block(t, quad), 1, 0)
        acc_v[window, cols] += dot(weights, grads, 1, 0)

        first = jnp.where(i % 2 == 0, TILE * (i // 2), EXT - TILE - TILE * (i // 2))
        done = pl.ds(pl.multiple_of(first, TILE), TILE)
        sbuf[i, 0, :, cols] = acc_k[done, cols].astype(BF16)
        sbuf[i, 1, :, cols] = acc_v[done, cols].astype(BF16)

        @pl.when((i % 2 == 0) & has_lower)
        def _():
            return_copy(i, 0, quad, lower).start()
            return_copy(i, 1, quad, lower).start()

        @pl.when((i % 2 == 1) & has_upper)
        def _():
            return_copy(i, 0, quad, upper).start()
            return_copy(i, 1, quad, upper).start()

    def backward_tile(i, carry):
        t = tile_of(i)

        def pass_on(quad, inner):
            far_copy(i, quad).wait_recv()
            fwd_copy(i, quad).start()
            return inner

        lax.fori_loop(0, QUADS, pass_on, 0)
        sib_copy(i).wait_recv()

        def arrived(quad, inner):
            fwd_copy(i, quad).wait_recv()
            return inner

        lax.fori_loop(0, QUADS, arrived, 0)
        cohort = att[:, i].reshape(4 * TILE, WIDTH)
        rows = pl.ds(pl.multiple_of(t * TILE, TILE), TILE)

        total = jnp.zeros((TILE, WIDTH), F32)
        pieces = []
        for b in range(4):
            cols = slice(b * 256, b * 256 + 256)
            forecast = dot(cohort, w_s[:, cols], 1, 0).astype(BF16).astype(F32)
            resident = forecast[:TILE]
            couples = slope(resident - forecast[TILE : 2 * TILE])
            couples += slope(resident - forecast[2 * TILE : 3 * TILE])
            couples += slope(resident - forecast[3 * TILE :])
            truth = obs[rows, cols].astype(F32)
            pieces.append((slope(resident - truth) - couples * (1.0 / 3.0)).astype(BF16))
        field_grad = jnp.concatenate(pieces, axis=1)
        dout[...] = dot(field_grad, w_s[...], 1, 1).astype(BF16)

        def step(quad, inner):
            backward_quad(i, quad)
            return inner

        lax.fori_loop(0, QUADS, step, 0)
        return carry

    lax.fori_loop(0, TILES, backward_tile, 0)

    copies_out = [pltpu.make_async_copy(gq_s, gq_hbm.at[0], out_sem.at[0])]
    copies_out[0].start()

    for block, slot in ((2, 0), (1, 1), (3, 2), (0, 3)):
        source_exists = has_upper if slot % 2 == 0 else has_lower
        source = upper if slot % 2 == 0 else lower
        rows = slice(block * TILE, block * TILE + TILE)
        inner_rows = slice(REACH + block * TILE, REACH + block * TILE + TILE)

        def finish(quad, carry, slot=slot, source_exists=source_exists, source=source, rows=rows, inner_rows=inner_rows):
            @pl.when(source_exists)
            def _():
                return_copy(slot, 0, quad, source).wait_recv()
                return_copy(slot, 1, quad, source).wait_recv()

            cols = lanes_of(quad)
            gk_s[rows, cols] = (acc_k[inner_rows, cols] + rbuf[slot, 0, :, cols].astype(F32)).astype(BF16)
            gv_s[rows, cols] = (acc_v[inner_rows, cols] + rbuf[slot, 1, :, cols].astype(F32)).astype(BF16)
            return carry

        lax.fori_loop(0, QUADS, finish, 0)
        pair = [
            pltpu.make_async_copy(gk_s.at[rows], gk_hbm.at[0, rows], out_sem.at[1 + 2 * block]),
            pltpu.make_async_copy(gv_s.at[rows], gv_hbm.at[0, rows], out_sem.at[2 + 2 * block]),
        ]
        for cp in pair:
            cp.start()
        copies_out += pair

    for step in range(4):
        w_sent(step)
    w_sib_out.wait_send()

    def sent(quad, carry):
        @pl.when(has_upper)
        def _():
            halo(0, 0, quad).wait_send()
            halo(0, 1, quad).wait_send()

        @pl.when(has_lower)
        def _():
            halo(1, 0, quad).wait_send()
            halo(1, 1, quad).wait_send()

        for i in range(TILES):
            far_copy(i, quad).wait_send()
            fwd_copy(i, quad).wait_send()

            @pl.when(has_lower if i % 2 == 0 else has_upper)
            def _(i=i):
                device = lower if i % 2 == 0 else upper
                return_copy(i, 0, quad, device).wait_send()
                return_copy(i, 1, quad, device).wait_send()

        return carry

    lax.fori_loop(0, QUADS, sent, 0)
    for i in range(TILES):
        sib_copy(i).wait_send()
    for cp in copies_out:
        cp.wait()


def body(query_states, key_states, value_states, observed, closing_projector):
    dma = pltpu.SemaphoreType.DMA
    hbm = pl.BlockSpec(memory_space=pl.ANY)
    grad = jax.ShapeDtypeStruct((1, ROWS, WIDTH), BF16)
    vmem = pltpu.VMEM
    return pl.pallas_call(
        kernel,
        out_shape=(grad, grad, grad),
        in_specs=[hbm, hbm, hbm, hbm, pl.BlockSpec(memory_space=pltpu.VMEM)],
        out_specs=(hbm, hbm, hbm),
        scratch_shapes=[
            vmem((ROWS, WIDTH), BF16),
            vmem((EXT, WIDTH), BF16),
            vmem((EXT, WIDTH), BF16),
            vmem((ROWS, WIDTH), BF16),
            vmem((16, 128), F32),
            vmem((512, 16, 128), BF16),
            vmem((8192, 128), F32),
            vmem((WIDTH, WIDTH), BF16),
            vmem((4, TILES, TILE, WIDTH), BF16),
            vmem((TILES * QUADS, WIN, LANES), BF16),
            vmem((TILES * QUADS, LANES, 128), F32),
            vmem((TILES * QUADS, 8, LANES), F32),
            vmem((TILES, WIN, LANES), F32),
            vmem((TILE, WIDTH), BF16),
            vmem((EXT, WIDTH), F32),
            vmem((EXT, WIDTH), F32),
            vmem((TILES, 2, TILE, WIDTH), BF16),
            vmem((TILES, 2, TILE, WIDTH), BF16),
            vmem((ROWS, WIDTH), BF16),
            vmem((ROWS, WIDTH), BF16),
            vmem((ROWS, WIDTH), BF16),
            dma((4,)),
            dma((2, 2, QUADS)), dma((2, 2, QUADS)),
            dma((3,)), dma((3,)),
            dma((3,)), dma((3,)),
            dma((3,)), dma((3,)),
            dma((3,)), dma((3,)),
            dma, dma,
            dma((TILES, QUADS)), dma((TILES, QUADS)),
            dma((TILES,)), dma((TILES,)),
            dma((TILES, QUADS)), dma((TILES, QUADS)),
            dma((TILES, 2, QUADS)), dma((TILES, 2, QUADS)),
            dma((9,)),
        ],
        compiler_params=pltpu.CompilerParams(
            collective_id=0, has_side_effects=True, vmem_limit_bytes=50 * 1024 * 1024
        ),
        name="window_backward",
    )(query_states, key_states, value_states, observed, closing_projector)


def solution(mesh):
    placed = (
        P("mem", "tok", None),
        P("mem", "tok", None),
        P("mem", "tok", None),
        P("tok", None),
        P(("tok", "mem"), None),
    )
    return jax.shard_map(
        body,
        mesh=mesh,
        in_specs=placed,
        out_specs=(P("mem", "tok", None), P("mem", "tok", None), P("mem", "tok", None)),
        check_vma=False,
    )
```

time: 926 us -> 118 us (0.13)
  the two profiles are of different devices: /device:TPU:126 before, /device:TPU:384 now
where the time goes in v1:
time: 118 us; the launch traced here: 117 us
  Pallas kernels  109 us (92%)
  local copies, waits for them, and re-layouts  7.23 us (6%)
    pallas_call x1, Pallas kernels, body(): pl.pallas_call(kernel, out_shape=(grad, grad, grad), in_specs=[hbm, hbm,...  109 us
    unnamed x13, local copies, waits for them, and re-layouts  7.23 us

profile of v1, /device:TPU:384, one launch (start us, length us, event | category | flops | bytes accessed | tf_op | source)
XLA Modules:
  0.0 116.8 jit_solution(3386998349048798092)
XLA Ops:
  0.6 0.0 copy-start
  0.6 1.0 copy-done
  1.7 0.0 copy-start.1
  1.7 1.0 copy-done.1
  2.7 0.0 copy-start.2
  2.7 1.0 copy-done.2
  3.8 0.0 copy-start.3
  3.8 1.0 copy-done.3
  4.8 0.0 copy-start.4
  4.8 0.7 copy-done.4
  5.5 109.0 %window_backward.1 = (bf16[1,256,1024]{2,1,0:T(8,128)(2,1)S(1)}, bf16[1,256,1024]{2,1,0:T(8,128)(2,1)S(1)}, bf16[1,256,1024]{2,1,0:T(8,128)(2,1)S(1)}) custom-call(bf16[1,256,1024]{2,1,0:T(8,128)(2,1)S(1)} %copy-done, bf16[1,256,1024]{2,1,0:T(8,128)(2,1)S(1)} %copy-done.1, bf16[1,256,1024]{2,1,0:T(8,128)(2,1)S(1)} %copy-done.2, ...), custom_call_target="tpu_custom_call" | custom-call | tf_op jit(solution)/shard_map/window_backward/pallas_call | solution.py:487
  114.5 0.8 copy.11
  115.3 0.8 copy.12
  116.0 0.8 copy.13
Async XLA Ops:
  0.6 1.0 copy-start
  1.7 1.0 copy-start.1
  2.7 1.0 copy-start.2
  3.8 1.0 copy-start.3
  4.8 0.7 copy-start.4

commit v2 on v1

--- a/solution.py
+++ b/solution.py
@@ -44,7 +44,7 @@
     gq_hbm, gk_hbm, gv_hbm,
     q_s, kx, vx, obs, w_tmp, wg, wf, w_s, att, probs, rl_rows, rl_lanes, bias,
     dout, acc_k, acc_v, sbuf, rbuf, gq_s, gk_s, gv_s,
-    load_sem, halo_ss, halo_rs, wz_ss, wz_rs, wn_ss, wn_rs, wy_ss, wy_rs, wx_ss, wx_rs, wc_ss, wc_rs,
+    load_sem, halo_ss, halo_rs, wz_ss, wz_rs, wy_ss, wy_rs, wx_ss, wx_rs, wc_ss, wc_rs,
     far_ss, far_rs, sib_ss, sib_rs, fwd_ss, fwd_rs, ret_ss, ret_rs, out_sem,
 ):
     tok = lax.axis_index("tok")
@@ -71,11 +71,13 @@
         pl.semaphore_signal(barrier, inc=1, device_id=device, device_id_type=MESH)
 
     greet(sibling)
+    for d in range(1, 16):
+        greet(chip(x, y, (z + d) % 16, c))
     for d in (1, 2, 3):
-        greet(chip(x, y, (z + 4 * d) % 16, c))
-        greet(chip(x, y, (z + 16 - d) % 16, c))
         greet(chip(x, (y + d) % 4, z, c))
         greet(chip((x + d) % 4, y, z, c))
+
+    first = tok % 16 == 0
 
     @pl.when(has_lower)
     def _():
@@ -99,60 +101,70 @@
     for r in range(2):
         for b in range(8):
             w_tmp[r * 8 + b : r * 8 + b + 1, :] = mine[r : r + 1, b * 128 : (b + 1) * 128]
-    unit = ((c * 4 + x) * 4 + y) * 16 + (z % 4) * 4 + z // 4
+    unit = ((c * 4 + x) * 4 + y) * 16 + z
     wg[unit] = w_tmp[...].astype(BF16)
 
+    def one(flag):
+        return jnp.where(flag, 1, 0)
+
     pl.semaphore_wait(
-        barrier, 13 + jnp.where(has_lower, 1, 0) + jnp.where(has_upper, 1, 0)
+        barrier,
+        22 + one(has_lower) + one(has_upper),
     )
 
+    def halo_parts(side, kv, quad):
+        ref = (kx, vx)[kv]
+        source = pl.ds(ROWS, REACH) if side == 0 else pl.ds(REACH, REACH)
+        target = pl.ds(0, REACH) if side == 0 else pl.ds(REACH + ROWS, REACH)
+        return ref.at[source, lanes_of(quad)], ref.at[target, lanes_of(quad)]
+
     def halo(side, kv, quad):
-        src = (k_hbm, v_hbm)[kv]
-        dst = (kx, vx)[kv]
-        cols = lanes_of(quad)
-        if side == 0:
-            return remote(
-                src.at[0, pl.ds(ROWS - REACH, REACH), cols], dst.at[pl.ds(0, REACH), cols],
-                halo_ss.at[0, kv, quad], halo_rs.at[0, kv, quad], upper,
-            )
+        src, dst = halo_parts(side, kv, quad)
         return remote(
-            src.at[0, pl.ds(0, REACH), cols], dst.at[pl.ds(REACH + ROWS, REACH), cols],
-            halo_ss.at[1, kv, quad], halo_rs.at[1, kv, quad], lower,
+            src, dst, halo_ss.at[side, kv, quad], halo_rs.at[side, kv, quad], upper if side == 0 else lower
         )
 
     def start_halo(quad, carry):
-        @pl.when(has_upper)
-        def _():
-            halo(0, 0, quad).start()
-            halo(0, 1, quad).start()
-
-        @pl.when(has_lower)
-        def _():
-            halo(1, 0, quad).start()
-            halo(1, 1, quad).start()
-
-        return carry
-
-    lax.fori_loop(0, QUADS, start_halo, 0)
+        for kv in range(2):
+
+            @pl.when(has_upper)
+            def _(kv=kv):
+                halo(0, kv, quad).start()
+
+            @pl.when(has_lower)
+            def _(kv=kv):
+                halo(1, kv, quad).start()
+
+        return carry
+
+    def halos_sent():
+        def step(quad, carry):
+            for kv in range(2):
+
+                @pl.when(has_upper)
+                def _(kv=kv):
+                    halo(0, kv, quad).wait_send()
+
+                @pl.when(has_lower)
+                def _(kv=kv):
+                    halo(1, kv, quad).wait_send()
+
+            return carry
+
+        lax.fori_loop(0, QUADS, step, 0)
 
     def w_copy(first, count, ss, rs, device):
         block = wg.at[pl.ds(first, count)]
         return remote(block, block, ss, rs, device)
 
     def w_step(step, d, incoming):
-        away = (z + 16 - 4 * d) % 16 if step == 0 else (z + 16 - d) % 16
-        away = away if incoming else z
-        plane = ((c * 4 + x) * 4 + y) * 16
         if step == 0:
+            level = (z + 16 - d) % 16 if incoming else z
             return w_copy(
-                plane + (away % 4) * 4 + away // 4, 1, wz_ss.at[d - 1], wz_rs.at[d - 1],
-                chip(x, y, (z + 4 * d) % 16, c),
+                ((c * 4 + x) * 4 + y) * 16 + level, 1, wz_ss.at[d - 1], wz_rs.at[d - 1],
+                chip(x, y, (z + d) % 16, c),
             )
         if step == 1:
-            return w_copy(
-                plane + (away % 4) * 4, 4, wn_ss.at[d - 1], wn_rs.at[d - 1], chip(x, y, (z + d) % 16, c)
-            )
-        if step == 2:
             column = (y + 4 - d) % 4 if incoming else y
             return w_copy(
                 ((c * 4 + x) * 4 + column) * 16, 16, wy_ss.at[d - 1], wy_rs.at[d - 1],
@@ -163,22 +175,28 @@
             (c * 4 + column) * 64, 64, wx_ss.at[d - 1], wx_rs.at[d - 1], chip((x + d) % 4, y, z, c)
         )
 
+    def w_offsets(step):
+        return range(1, 16 if step == 0 else 4)
+
     def w_start(step):
-        for d in (1, 2, 3):
+        for d in w_offsets(step):
             w_step(step, d, False).start()
 
     def w_wait(step):
-        for d in (1, 2, 3):
+        for d in w_offsets(step):
             w_step(step, d, True).wait_recv()
 
     def w_sent(step):
-        for d in (1, 2, 3):
+        for d in w_offsets(step):
             w_step(step, d, False).wait_send()
 
     w_sib_out = w_copy(c * 256, 256, wc_ss, wc_rs, sibling)
     w_sib_in = w_copy((1 - c) * 256, 256, wc_ss, wc_rs, sibling)
 
     w_start(0)
+    loads[0].wait()
+    loads[2].wait()
+    lax.fori_loop(0, QUADS, start_halo, 0)
 
     row = lax.broadcasted_iota(jnp.int32, (WIN, LANES), 0)
     query = lax.broadcasted_iota(jnp.int32, (WIN, LANES), 1) % TILE
@@ -212,9 +230,8 @@
         for slot in (0, 2):
             rbuf[slot] = jnp.zeros((2, TILE, WIDTH), BF16)
 
-    for cp in loads:
-        cp.wait()
-
+    loads[1].wait()
+    loads[3].wait()
     left_half = lax.broadcasted_iota(jnp.int32, (TILE, 128), 1) < HD
 
     def spread(pairs):
@@ -226,8 +243,15 @@
             rows.append(jnp.concatenate([part, none] if h < 2 else [none, part], axis=1))
         return jnp.concatenate(rows, axis=0).astype(BF16)
 
+    mirrored = jnp.where(first, 1, 0)
+
     def tile_of(i):
-        return i // 2 + (i % 2) * (3 - 2 * (i // 2))
+        t = i + (i // 2) * (5 - 2 * i)
+        return t + mirrored * (3 - 2 * t)
+
+    def slot_of(i):
+        slot = (i % 2) * 2 + i // 2
+        return slot + mirrored * (1 - 2 * (slot % 2))
 
     def query_block(t, quad):
         rows = pl.ds(pl.multiple_of(t * TILE, TILE), TILE)
@@ -250,12 +274,12 @@
     def forward_quad(i, quad):
         t = tile_of(i)
 
-        @pl.when((i == 0) & has_lower)
+        @pl.when((slot_of(i) == 0) & has_lower)
         def _():
             halo(0, 0, quad).wait_recv()
             halo(0, 1, quad).wait_recv()
 
-        @pl.when((i == 1) & has_upper)
+        @pl.when((slot_of(i) == 1) & has_upper)
         def _():
             halo(1, 0, quad).wait_recv()
             halo(1, 1, quad).wait_recv()
@@ -300,24 +324,27 @@
             w_wait(1)
             w_start(2)
 
-        @pl.when(i == 2)
-        def _():
-            w_wait(2)
-            w_start(3)
-
         return carry
 
     lax.fori_loop(0, TILES, forward_tile, 0)
 
-    w_wait(3)
+    def pass_on(i):
+        def step(quad, inner):
+            far_copy(i, quad).wait_recv()
+            fwd_copy(i, quad).start()
+            return inner
+
+        lax.fori_loop(0, QUADS, step, 0)
+
+    pass_on(0)
+    w_wait(2)
     w_sib_out.start()
     w_sib_in.wait_recv()
 
     def place_units(n, carry):
-        for zr in range(4):
-            for zq in range(4):
-                d = ((zq % 2) * 4 + zr) * 64 + (n % 16) * 4 + (zq // 2) * 2 + n // 16
-                wf[pl.ds(pl.multiple_of(d * 16, 16), 16), :] = wg[n * 16 + zr * 4 + zq].astype(F32)
+        for level in range(16):
+            d = (level % 8) * 64 + (n % 16) * 4 + (level // 8) * 2 + n // 16
+            wf[pl.ds(pl.multiple_of(d * 16, 16), 16), :] = wg[n * 16 + level].astype(F32)
         return carry
 
     lax.fori_loop(0, 32, place_units, 0)
@@ -334,6 +361,17 @@
     def return_copy(i, kv, quad, device):
         cols = lanes_of(quad)
         return remote(sbuf.at[i, kv, :, cols], rbuf.at[i, kv, :, cols], ret_ss.at[i, kv, quad], ret_rs.at[i, kv, quad], device)
+
+    def start_return(slot, quad):
+        for kv in range(2):
+
+            @pl.when((slot % 2 == 0) & has_lower)
+            def _(kv=kv):
+                return_copy(slot, kv, quad, lower).start()
+
+            @pl.when((slot % 2 == 1) & has_upper)
+            def _(kv=kv):
+                return_copy(slot, kv, quad, upper).start()
 
     def backward_quad(i, quad):
         t = tile_of(i)
@@ -359,30 +397,20 @@
         acc_k[window, cols] += dot(score_grad, query_block(t, quad), 1, 0)
         acc_v[window, cols] += dot(weights, grads, 1, 0)
 
-        first = jnp.where(i % 2 == 0, TILE * (i // 2), EXT - TILE - TILE * (i // 2))
-        done = pl.ds(pl.multiple_of(first, TILE), TILE)
-        sbuf[i, 0, :, cols] = acc_k[done, cols].astype(BF16)
-        sbuf[i, 1, :, cols] = acc_v[done, cols].astype(BF16)
-
-        @pl.when((i % 2 == 0) & has_lower)
-        def _():
-            return_copy(i, 0, quad, lower).start()
-            return_copy(i, 1, quad, lower).start()
-
-        @pl.when((i % 2 == 1) & has_upper)
-        def _():
-            return_copy(i, 0, quad, upper).start()
-            return_copy(i, 1, quad, upper).start()
+        slot = slot_of(i)
+        first_row = jnp.where(slot % 2 == 0, TILE * (slot // 2), EXT - TILE - TILE * (slot // 2))
+        done = pl.ds(pl.multiple_of(first_row, TILE), TILE)
+        sbuf[slot, 0, :, cols] = acc_k[done, cols].astype(BF16)
+        sbuf[slot, 1, :, cols] = acc_v[done, cols].astype(BF16)
+        start_return(slot, quad)
 
     def backward_tile(i, carry):
         t = tile_of(i)
 
-        def pass_on(quad, inner):
-            far_copy(i, quad).wait_recv()
-            fwd_copy(i, quad).start()
-            return inner
-
-        lax.fori_loop(0, QUADS, pass_on, 0)
+        @pl.when(i > 0)
+        def _():
+            pass_on(i)
+
         sib_copy(i).wait_recv()
 
         def arrived(quad, inner):
@@ -390,6 +418,7 @@
             return inner
 
         lax.fori_loop(0, QUADS, arrived, 0)
+
         cohort = att[:, i].reshape(4 * TILE, WIDTH)
         rows = pl.ds(pl.multiple_of(t * TILE, TILE), TILE)
 
@@ -412,6 +441,7 @@
             return inner
 
         lax.fori_loop(0, QUADS, step, 0)
+
         return carry
 
     lax.fori_loop(0, TILES, backward_tile, 0)
@@ -445,21 +475,13 @@
             cp.start()
         copies_out += pair
 
-    for step in range(4):
+    for step in range(3):
         w_sent(step)
     w_sib_out.wait_send()
 
+    halos_sent()
+
     def sent(quad, carry):
-        @pl.when(has_upper)
-        def _():
-            halo(0, 0, quad).wait_send()
-            halo(0, 1, quad).wait_send()
-
-        @pl.when(has_lower)
-        def _():
-            halo(1, 0, quad).wait_send()
-            halo(1, 1, quad).wait_send()
-
         for i in range(TILES):
             far_copy(i, quad).wait_send()
             fwd_copy(i, quad).wait_send()
@@ -475,20 +497,21 @@
     lax.fori_loop(0, QUADS, sent, 0)
     for i in range(TILES):
         sib_copy(i).wait_send()
+
     for cp in copies_out:
         cp.wait()
 
 
 def body(query_states, key_states, value_states, observed, closing_projector):
     dma = pltpu.SemaphoreType.DMA
-    hbm = pl.BlockSpec(memory_space=pl.ANY)
+    hbm = pl.BlockSpec(memory_space=pltpu.HBM)
     grad = jax.ShapeDtypeStruct((1, ROWS, WIDTH), BF16)
     vmem = pltpu.VMEM
     return pl.pallas_call(
         kernel,
         out_shape=(grad, grad, grad),
-        in_specs=[hbm, hbm, hbm, hbm, pl.BlockSpec(memory_space=pltpu.VMEM)],
-        out_specs=(hbm, hbm, hbm),
+        in_specs=[hbm] * 4 + [pl.BlockSpec(memory_space=pltpu.VMEM)],
+        out_specs=(pl.BlockSpec(memory_space=pl.ANY),) * 3,
         scratch_shapes=[
             vmem((ROWS, WIDTH), BF16),
             vmem((EXT, WIDTH), BF16),
@@ -513,8 +536,7 @@
             vmem((ROWS, WIDTH), BF16),
             dma((4,)),
             dma((2, 2, QUADS)), dma((2, 2, QUADS)),
-            dma((3,)), dma((3,)),
-            dma((3,)), dma((3,)),
+            dma((15,)), dma((15,)),
             dma((3,)), dma((3,)),
             dma((3,)), dma((3,)),
             dma, dma,
@@ -525,7 +547,7 @@
             dma((9,)),
         ],
         compiler_params=pltpu.CompilerParams(
-            collective_id=0, has_side_effects=True, vmem_limit_bytes=50 * 1024 * 1024
+            collective_id=0, has_side_effects=True, vmem_limit_bytes=56 * 1024 * 1024
         ),
         name="window_backward",
     )(query_states, key_states, value_states, observed, closing_projector)

time: 118 us -> 105 us (0.89)
  Pallas kernels: 109 us -> 100 us
  local copies, waits for them, and re-layouts: 7.23 us -> 3.95 us
    pallas_call x1, Pallas kernels: 109 us -> 100 us  [body(): pl.pallas_call(kernel, out_shape=(grad, grad, grad), in_specs=[hbm] * 4 +...]
    unnamed x13 -> x7, local copies, waits for them, and re-layouts: 7.23 us -> 3.95 us
where the time goes in v2:
time: 105 us
  Pallas kernels  100 us (95%)
  local copies, waits for them, and re-layouts  3.95 us (4%)
    pallas_call x1, Pallas kernels, body(): pl.pallas_call(kernel, out_shape=(grad, grad, grad), in_specs=[hbm] * 4 +...  100 us
    unnamed x7, local copies, waits for them, and re-layouts  3.95 us

profile of v2, /device:TPU:384, one launch (start us, length us, event | category | flops | bytes accessed | tf_op | source)
XLA Modules:
  0.0 104.9 jit_solution(15499897678570071494)
XLA Ops:
  0.6 100.3 %window_backward.1 = (bf16[1,256,1024]{2,1,0:T(8,128)(2,1)}, bf16[1,256,1024]{2,1,0:T(8,128)(2,1)}, bf16[1,256,1024]{2,1,0:T(8,128)(2,1)}) custom-call(bf16[1,256,1024]{2,1,0:T(8,128)(2,1)} %q_hbm.1, bf16[1,256,1024]{2,1,0:T(8,128)(2,1)} %k_hbm.1, bf16[1,256,1024]{2,1,0:T(8,128)(2,1)} %v_hbm.1, bf16[256,1024]{1,0:T(8,128)(2,1)} %o_hbm.1, bf16[2,1024]{1,0:T(2,128)(2,1)} %w_in.1), custom_call_target="tpu_custom_call" | custom-call | tf_op jit(solution)/shard_map/window_backward/pallas_call | solution.py:510
  100.9 0.0 copy-start.1
  100.9 1.9 %copy.11 = bf16[1,256,1024]{2,1,0:T(8,128)(2,1)} copy(bf16[1,256,1024]{2,1,0:T(8,128)(2,1)} %get-tuple-element.6) | data formatting | bytes 1048576
  102.9 0.0 copy-done.1
  102.9 0.0 copy-start
  102.9 0.8 copy.12
  103.7 0.4 copy-done
  104.1 0.8 copy.13
Async XLA Ops:
  100.9 1.9 %copy-start.1 = (bf16[1,256,1024]{2,1,0:T(8,128)(2,1)S(1)}, bf16[1,256,1024]{2,1,0:T(8,128)(2,1)}, u32[]{:S(2)}) copy-start(bf16[1,256,1024]{2,1,0:T(8,128)(2,1)} %get-tuple-element.7) | copy-start | bytes 1572868
  102.9 1.2 %copy-start = (bf16[1,256,1024]{2,1,0:T(8,128)(2,1)S(1)}, bf16[1,256,1024]{2,1,0:T(8,128)(2,1)}, u32[]{:S(2)}) copy-start(bf16[1,256,1024]{2,1,0:T(8,128)(2,1)} %get-tuple-element.8) | copy-start | bytes 1572868

commit v3 on v2

--- a/solution.py
+++ b/solution.py
@@ -386,6 +386,16 @@
         wide = weights.astype(F32)
         row_dot = jnp.sum(wide * prob_grad, axis=0, keepdims=True) * rl_lanes[n, 0:1, :]
         score_grad = (wide * (prob_grad - row_dot)).astype(BF16)
+        acc_k[window, cols] += dot(score_grad, query_block(t, quad), 1, 0)
+        acc_v[window, cols] += dot(weights, grads, 1, 0)
+
+        slot = slot_of(i)
+        first_row = jnp.where(slot % 2 == 0, TILE * (slot // 2), EXT - TILE - TILE * (slot // 2))
+        done = pl.ds(pl.multiple_of(first_row, TILE), TILE)
+        sbuf[slot, 0, :, cols] = acc_k[done, cols].astype(BF16)
+        sbuf[slot, 1, :, cols] = acc_v[done, cols].astype(BF16)
+        start_return(slot, quad)
+
         keys = kx[window, cols]
         halves = []
         for half in range(2):
@@ -394,15 +404,6 @@
             halves.append(jnp.where(left_half, mixed[:TILE], mixed[TILE:]))
         rows = pl.ds(pl.multiple_of(t * TILE, TILE), TILE)
         gq_s[rows, cols] = jnp.concatenate(halves, axis=1).astype(BF16)
-        acc_k[window, cols] += dot(score_grad, query_block(t, quad), 1, 0)
-        acc_v[window, cols] += dot(weights, grads, 1, 0)
-
-        slot = slot_of(i)
-        first_row = jnp.where(slot % 2 == 0, TILE * (slot // 2), EXT - TILE - TILE * (slot // 2))
-        done = pl.ds(pl.multiple_of(first_row, TILE), TILE)
-        sbuf[slot, 0, :, cols] = acc_k[done, cols].astype(BF16)
-        sbuf[slot, 1, :, cols] = acc_v[done, cols].astype(BF16)
-        start_return(slot, quad)
 
     def backward_tile(i, carry):
         t = tile_of(i)
@@ -440,7 +441,7 @@
             backward_quad(i, quad)
             return inner
 
-        lax.fori_loop(0, QUADS, step, 0)
+        lax.fori_loop(0, QUADS, step, 0, unroll=2)
 
         return carry
 

time: 105 us -> 106 us (level)
  no operation moved by 1% of the time
where the time goes in v3:
time: 106 us; the launch traced here: 105 us
  Pallas kernels  101 us (95%)
  local copies, waits for them, and re-layouts  3.95 us (4%)
    pallas_call x1, Pallas kernels, body(): pl.pallas_call(kernel, out_shape=(grad, grad, grad), in_specs=[hbm] * 4 +...  101 us
    unnamed x7, local copies, waits for them, and re-layouts  3.95 us

profile of v3, /device:TPU:384, one launch (start us, length us, event | category | flops | bytes accessed | tf_op | source)
XLA Modules:
  0.0 105.3 jit_solution(17129715120822451222)
XLA Ops:
  0.6 100.7 %window_backward.1 = (bf16[1,256,1024]{2,1,0:T(8,128)(2,1)}, bf16[1,256,1024]{2,1,0:T(8,128)(2,1)}, bf16[1,256,1024]{2,1,0:T(8,128)(2,1)}) custom-call(bf16[1,256,1024]{2,1,0:T(8,128)(2,1)} %q_hbm.1, bf16[1,256,1024]{2,1,0:T(8,128)(2,1)} %k_hbm.1, bf16[1,256,1024]{2,1,0:T(8,128)(2,1)} %v_hbm.1, bf16[256,1024]{1,0:T(8,128)(2,1)} %o_hbm.1, bf16[2,1024]{1,0:T(2,128)(2,1)} %w_in.1), custom_call_target="tpu_custom_call" | custom-call | tf_op jit(solution)/shard_map/window_backward/pallas_call | solution.py:511
  101.4 0.0 copy-start.1
  101.4 1.9 %copy.11 = bf16[1,256,1024]{2,1,0:T(8,128)(2,1)} copy(bf16[1,256,1024]{2,1,0:T(8,128)(2,1)} %get-tuple-element.6) | data formatting | bytes 1048576
  103.3 0.0 copy-done.1
  103.3 0.0 copy-start
  103.3 0.8 copy.12
  104.1 0.4 copy-done
  104.5 0.8 copy.13
Async XLA Ops:
  101.4 1.9 %copy-start.1 = (bf16[1,256,1024]{2,1,0:T(8,128)(2,1)S(1)}, bf16[1,256,1024]{2,1,0:T(8,128)(2,1)}, u32[]{:S(2)}) copy-start(bf16[1,256,1024]{2,1,0:T(8,128)(2,1)} %get-tuple-element.7) | copy-start | bytes 1572868
  103.3 1.2 %copy-start = (bf16[1,256,1024]{2,1,0:T(8,128)(2,1)S(1)}, bf16[1,256,1024]{2,1,0:T(8,128)(2,1)}, u32[]{:S(2)}) copy-start(bf16[1,256,1024]{2,1,0:T(8,128)(2,1)} %get-tuple-element.8) | copy-start | bytes 1572868
